TPU v7x, 128 devices: a whole 4x4x4 slice. The times are simulated.
128 devices in a mesh: dp: 32 (over z, x_lo, y), pair: 4 (over x_hi, core).
Axes of the slice: x: 4 (x_hi: 2, x_lo: 2; x = x_hi * 2 + x_lo), y: 4, z: 4, core: 2. Of those that a mesh axis runs over, the one named last changes fastest.
Arguments:
- protein: float32 [16384, 1024], P(('dp', 'pair')), may hold values from -6 to 6
- text: float32 [16384, 1024], P(('dp', 'pair')), may hold values from -6 to 6
- scale: float32 [], replicated, may hold values from 5 to 15
- bias: float32 [], replicated, may hold values from -4 to -2
Outputs:
- grad_protein: float32 [16384, 1024], P(('dp', 'pair'))
- grad_text: float32 [16384, 1024], P(('dp', 'pair'))
All inputs are finite; a program needn't handle non-finite values.
Results may differ from a plain program's by a relative error of at most 0.006.
Values may be sent and summed in bfloat16 or wider, within the bound.
A program may use at most 64 MiB of HBM per device.

v0:
```python
import jax
import jax.numpy as jnp
from jax import lax
from jax.sharding import PartitionSpec as P


def unit_rows(values):
    norm = jnp.sqrt(jnp.sum(values * values, axis=1, keepdims=True) + 1e-06)
    return (values / norm, norm)


def back_norm(grad_unit, unit, norm):
    inner = jnp.sum(unit * grad_unit, axis=1, keepdims=True)
    return (grad_unit - unit * inner) / norm


def on_device(protein, text, scale, bias):
    rows_dev = protein.shape[0]
    pair_count = lax.axis_size("pair")
    dp_index = lax.axis_index("dp")
    pair_index = lax.axis_index("pair")
    unit_p, norm_p = unit_rows(protein)
    unit_q, norm_q = unit_rows(text)
    unit_pb = unit_p.astype(jnp.bfloat16)
    unit_qb = unit_q.astype(jnp.bfloat16)
    rows_b = lax.all_gather(unit_pb, "pair", axis=0, tiled=True)
    row_global = dp_index * (pair_count * rows_dev) + jnp.arange(
        pair_count * rows_dev, dtype=jnp.int32
    )
    columns = lax.all_gather(unit_qb, "dp", axis=0, tiled=True)
    local = jnp.arange(columns.shape[0], dtype=jnp.int32)
    col_global = (local // rows_dev * pair_count + pair_index) * rows_dev + local % rows_dev
    logit = scale * jnp.dot(rows_b, columns.T, preferred_element_type=jnp.float32) + bias
    sign = jnp.where(row_global[:, None] == col_global[None, :], 1.0, -1.0).astype(jnp.float32)
    coef = (-sign * jax.nn.sigmoid(-sign * logit) * scale).astype(jnp.bfloat16)
    partial_p = jnp.dot(coef, columns, preferred_element_type=jnp.float32)
    partial_q = lax.dot_general(
        coef, rows_b, (((0,), (0,)), ((), ())), preferred_element_type=jnp.float32
    )
    grad_unit_q = lax.psum_scatter(partial_q, "dp", scatter_dimension=0, tiled=True)
    grad_unit_p = lax.psum_scatter(partial_p, "pair", scatter_dimension=0, tiled=True)
    return (back_norm(grad_unit_p, unit_p, norm_p), back_norm(grad_unit_q, unit_q, norm_q))


def solution(mesh):
    in_specs = (P(("dp", "pair"), None), P(("dp", "pair"), None), P(), P())
    out_specs = (P(("dp", "pair"), None), P(("dp", "pair"), None))
    return jax.shard_map(
        on_device, mesh=mesh, in_specs=in_specs, out_specs=out_specs, check_vma=False
    )
```

profile of v0, /device:TPU:0, one launch (start us, length us, event | category | flops | bytes accessed | tf_op | source)
XLA Modules:
  0.0 474.6 jit_solution(8700370713970205777)
XLA Ops:
  7.2 0.0 all-gather.3.cloned.1.call-start
  7.2 1.2 multiply_reduce_fusion.3
  8.4 1.9 fusion.11
  10.2 0.0 all-gather.3.cloned.1.call-update
  10.3 0.0 all-gather.5.cloned.1.call-start
  10.3 1.2 multiply_reduce_fusion.2
  11.5 1.9 fusion.12
  13.3 0.0 all-gather.5.cloned.1.call-update
  13.4 0.0 reduce-scatter.3.cloned.1.call-start
  14.8 18.9 %all-gather.3.cloned.1.call-done = bf16[512,1024]{1,0:T(8,128)(2,1)} async-done(((bf16[128,1024]{1,0:T(8,128)(2,1)}), bf16[512,1024]{1,0:T(8,128)(2,1)}) %all-gather.3.cloned.1.call-update) | async-done | bytes 1048592 | tf_op jit(solution)/shard_map/all_gather | solution.py:26
  33.6 169.0 %all-gather.5.cloned.1.call-done = bf16[4096,1024]{1,0:T(8,128)(2,1)} async-done(((bf16[128,1024]{1,0:T(8,128)(2,1)}), bf16[4096,1024]{1,0:T(8,128)(2,1)}) %all-gather.5.cloned.1.call-update) | async-done | bytes 8388624 | tf_op jit(solution)/shard_map/all_gather | solution.py:30
  202.6 0.0 copy-start.2
  202.6 10.3 %multiply_convert_fusion = bf16[512,4096]{1,0:T(8,128)(2,1)S(1)} fusion(bf16[512,1024]{1,0:T(8,128)(2,1)} %all-gather.3.cloned.1.call-done, bf16[4096,1024]{1,0:T(8,128)(2,1)} %all-gather.5.cloned.1.call-done, f32[]{:T(128)S(6)} %copy.7, f32[]{:T(128)S(6)} %copy.6, s32[4096]{0:T(1024)S(1)} %fusion.9, s32[512]{0:T(512)S(1)} %iota_add_fusion), kind=kOutput, calls=%fused_computation | convolution fusion | flops 4320133120 | bytes 13649928 | tf_op jit(solution)/shard_map/dot_general | solution.py:33
  212.9 0.0 copy-start.4
  212.9 1.9 copy-done.4
  214.8 0.0 copy-done.2
  214.8 0.0 copy-start.3
  214.8 5.9 %fusion.13 = f32[512,1024]{1,0:T(8,128)} fusion(bf16[512,4096]{1,0:T(8,128)(2,1)S(1)} %multiply_convert_fusion, bf16[4096,1024]{1,0:T(8,128)(2,1)S(1)} %copy-done.2), kind=kOutput, calls=%fused_computation.29 | convolution fusion | flops 4294967296 | bytes 14680064 | tf_op jit(solution)/shard_map/dot_general | solution.py:36
  220.7 0.0 reduce-scatter.3.cloned.1.call-update
  220.7 0.0 reduce-scatter.5.cloned.1.call-start
  220.7 0.0 copy-done.3
  220.8 10.7 %fusion.14 = f32[4096,1024]{1,0:T(8,128)} fusion(bf16[512,4096]{1,0:T(8,128)(2,1)} %copy-done.4, bf16[512,1024]{1,0:T(8,128)(2,1)S(1)} %copy-done.3), kind=kOutput, calls=%fused_computation.30 | convolution fusion | flops 4294967296 | bytes 22020096 | tf_op jit(solution)/shard_map/dot_general | solution.py:37
  231.4 0.0 copy-start
  231.4 0.0 copy-start.1
  231.4 0.0 reduce-scatter.5.cloned.1.call-update
  231.4 28.2 %reduce-scatter.3.cloned.1.call-done = f32[128,1024]{1,0:T(8,128)} async-done(((f32[512,1024]{1,0:T(8,128)}), f32[128,1024]{1,0:T(8,128)}) %reduce-scatter.3.cloned.1.call-update) | async-done | bytes 524304 | tf_op jit(solution)/shard_map/reduce_scatter | solution.py:41
  259.7 0.0 copy-done
  259.7 1.3 multiply_reduce_fusion.1
  260.9 2.0 subtract_divide_fusion.1
  262.9 201.9 %reduce-scatter.5.cloned.1.call-done = f32[128,1024]{1,0:T(8,128)} async-done(((f32[4096,1024]{1,0:T(8,128)}), f32[128,1024]{1,0:T(8,128)}) %reduce-scatter.5.cloned.1.call-update) | async-done | bytes 524304 | tf_op jit(solution)/shard_map/reduce_scatter | solution.py:40
  464.8 0.0 copy-done.1
  464.8 1.3 multiply_reduce_fusion
  466.1 2.0 subtract_divide_fusion
  (4 shorter events, 0.0 us)
Async XLA Ops:
  7.2 26.5 %all-gather.3.cloned.1.call-start = ((), (), s32[]{:S(2)}) async-start(), calls=%async_computation.2 | async-start | bytes 1310720 | tf_op jit(solution)/shard_map/all_gather | solution.py:26
  10.3 192.3 %all-gather.5.cloned.1.call-start = ((), (), s32[]{:S(2)}) async-start(), calls=%async_computation.3 | async-start | bytes 8650752 | tf_op jit(solution)/shard_map/all_gather | solution.py:30
  13.4 246.3 %reduce-scatter.3.cloned.1.call-start = ((), (), s32[]{:S(2)}) async-start(), calls=%async_computation.4 | async-start | bytes 2621440 | tf_op jit(solution)/shard_map/reduce_scatter | solution.py:41
  202.6 12.2 %copy-start.2 = (bf16[4096,1024]{1,0:T(8,128)(2,1)S(1)}, bf16[4096,1024]{1,0:T(8,128)(2,1)}, u32[]{:S(2)}) copy-start(bf16[4096,1024]{1,0:T(8,128)(2,1)} %all-gather.5.cloned.1.call-done) | copy-start | bytes 25165828
  212.9 1.9 copy-start.4
  214.8 5.9 %copy-start.3 = (bf16[512,1024]{1,0:T(8,128)(2,1)S(1)}, bf16[512,1024]{1,0:T(8,128)(2,1)}, u32[]{:S(2)}) copy-start(bf16[512,1024]{1,0:T(8,128)(2,1)} %all-gather.3.cloned.1.call-done) | copy-start | bytes 3145732
  220.7 244.2 %reduce-scatter.5.cloned.1.call-start = ((), (), s32[]{:S(2)}) async-start(), calls=%async_computation.5 | async-start | bytes 17301504 | tf_op jit(solution)/shard_map/reduce_scatter | solution.py:40
  231.4 28.2 %copy-start = (f32[128,1024]{1,0:T(8,128)S(1)}, f32[128,1024]{1,0:T(8,128)}, u32[]{:S(2)}) copy-start(f32[128,1024]{1,0:T(8,128)} %param.4) | copy-start | bytes 1572868
  231.4 233.4 %copy-start.1 = (f32[128,1024]{1,0:T(8,128)S(1)}, f32[128,1024]{1,0:T(8,128)}, u32[]{:S(2)}) copy-start(f32[128,1024]{1,0:T(8,128)} %param.5) | copy-start | bytes 1572868
Sparse Core Ops, SparseCore 0:
  10.4 23.1 all-gather.2
  35.8 166.7 all-gather.4
  220.8 38.8 reduce-scatter.2
  262.0 202.7 reduce-scatter.4
where the time goes:
time: 475 us
  waiting for transfers between devices  418 us (88%)
  matrix products  26.8 us (6%)
  between operations  15.1 us (3%)
  other arithmetic  12.6 us (3%)
    reduce_scatter x1, waiting for transfers between devices, on_device(): lax.psum_scatter(partial_q, 'dp', scatter_dimension=0, tiled=True)  202 us
    all_gather x1, waiting for transfers between devices, on_device(): columns = lax.all_gather(unit_qb, 'dp', axis=0, tiled=True)  169 us
    reduce_scatter x1, waiting for transfers between devices, on_device(): lax.psum_scatter(partial_p, 'pair', scatter_dimension=0, tiled=True)  28.2 us
    all_gather x1, waiting for transfers between devices, on_device(): rows_b = lax.all_gather(unit_pb, 'pair', axis=0, tiled=True)  18.9 us
    dot_general x1, matrix products, on_device(): lax.dot_general(coef, rows_b, (((0,), (0,)), ((), ())), preferred_element...  10.7 us
    dot_general x1, matrix products, on_device(): jnp.dot(rows_b, columns.T, preferred_element_type=jnp.float32)  10.3 us
  transfers between devices with their start and end apart: 4, of which 4 were waited for; matrix products, arithmetic and copies ran while one was open for 4% of the time, Pallas kernels for 0%

commit v1 on v0

v1 whole, which is shorter than its diff:
```python
import math

import jax
import jax.numpy as jnp
from jax import lax
from jax.experimental import pallas as pl
from jax.experimental.pallas import tpu as pltpu
from jax.sharding import PartitionSpec as P

MESH = pl.DeviceIdType.MESH
F32, BF16 = jnp.float32, jnp.bfloat16
LOG2E = math.log2(math.e)
WIDTH = 1024
ROWS = 128
BLOCK = 256
PARTS = ((0, 48, 0), (48, 48, 96), (96, 32, 192))
N_COPIES = 56


def neighbours():
    dp, pair = lax.axis_index("dp"), lax.axis_index("pair")
    z, x_lo, y = dp // 8, (dp // 4) % 2, dp % 4
    x_hi, core = pair // 2, pair % 2
    x = x_hi * 2 + x_lo

    def device(x, y, z, core):
        return (z * 8 + (x % 2) * 4 + y, (x // 2) * 2 + core)

    def p_flip(i):
        return i + 1 - 2 * (i % 2)

    def q_flip(i):
        return (i + 3 + 2 * (i % 2)) % 4

    def cube(flip):
        return (device(flip(x), y, z, core), device(x, flip(y), z, core), device(x, y, flip(z), core))

    return cube(p_flip), cube(q_flip), device(x, y, z, 1 - core)


def kernel(
    scale_ref, bias_ref, protein, text, out_p, out_q,
    unit_p, unit_q, norm_p, norm_q, rows_p, rows_q, coef, acc_p, acc_q, sib_out, sib_in,
    out1_p, out1_q, in1_p, in1_q, out2_p, out2_q, in2_p, in2_q, out3_p, out3_q, in3_p, in3_q,
    load_sem, send_sem, recv_sem,
):
    cube_p, cube_q, sibling = neighbours()
    barrier = pltpu.get_barrier_semaphore()
    for device in (*cube_p, *cube_q, sibling):
        pl.semaphore_signal(barrier, inc=1, device_id=device, device_id_type=MESH)
    load_p = pltpu.make_async_copy(protein, unit_p, load_sem.at[0])
    load_q = pltpu.make_async_copy(text, unit_q, load_sem.at[1])
    load_p.start()
    load_q.start()
    scale, bias = scale_ref[0], bias_ref[0]
    copies = []

    def send(src, dst, device):
        i = len(copies)
        copy = pltpu.make_async_remote_copy(
            src_ref=src, dst_ref=dst, send_sem=send_sem.at[i], recv_sem=recv_sem.at[i],
            device_id=device, device_id_type=MESH,
        )
        copy.start()
        copies.append(copy)
        return copy

    def normalise(load, unit, norm, rows):
        load.wait()
        values = unit[...]
        length = jnp.sqrt(jnp.sum(values * values, axis=1, keepdims=True) + 1e-06)
        values = values / length
        unit[...] = values
        norm[...] = length
        for first, size, offset in PARTS:
            rows[offset : offset + size, :] = values[first : first + size].astype(BF16)

    normalise(load_p, unit_p, norm_p, rows_p)
    normalise(load_q, unit_q, norm_q, rows_q)
    pl.semaphore_wait(barrier, 7)

    sides = ((rows_p, 512, cube_p), (rows_q, 256, cube_q))

    def gather(side, part, source, target, link):
        rows, stride, cube = sides[side]
        _, size, offset = PARTS[part]
        return send(
            rows.at[pl.ds(source * stride + offset, 2 * size)],
            rows.at[pl.ds(target * stride + offset, 2 * size)],
            cube[(part + link) % 3],
        )

    def to_sibling(block):
        return send(
            rows_p.at[pl.ds(block * 512, BLOCK)], rows_p.at[pl.ds(block * 512 + BLOCK, BLOCK)], sibling
        )

    both = [(side, part) for part in range(3) for side in range(2)]
    first = {}
    for side, part in both:
        rows, _, cube = sides[side]
        _, size, offset = PARTS[part]
        first[side, part] = send(
            rows.at[pl.ds(offset, size)], rows.at[pl.ds(offset + size, size)], cube[part]
        )
    second, third, fourth, siblings = {}, {}, {}, {}
    for side, part in both:
        first[side, part].wait_recv()
        second[side, part] = gather(side, part, 0, 1, 1)
    for side, part in both:
        third[side, part] = gather(side, part, 0, 2, 2)
    siblings[0] = to_sibling(0)

    def logits(row, size, block):
        return lax.dot_general(
            rows_p[row : row + size, :], rows_q[block * BLOCK : (block + 1) * BLOCK, :],
            (((1,), (1,)), ((), ())), preferred_element_type=F32,
        )

    slope, shift = scale * -LOG2E, bias * -LOG2E

    def fill(row, size, block):
        power = jnp.exp2(logits(row, size, block) * slope + shift)
        coef[row : row + size, block * BLOCK : (block + 1) * BLOCK] = (scale / (1.0 + power)).astype(BF16)

    def fill_own():
        values = scale * logits(0, BLOCK, 0) + bias
        row = lax.broadcasted_iota(jnp.int32, (BLOCK, BLOCK), 0)
        column = lax.broadcasted_iota(jnp.int32, (BLOCK, BLOCK), 1)
        own = (row < 48) | ((row >= 96) & (row < 144)) | ((row >= 192) & (row < 224))
        sign = jnp.where((row == column) & own, 1.0, -1.0)
        coef[0:BLOCK, 0:BLOCK] = (-sign * scale / (1.0 + jnp.exp2(sign * values * LOG2E))).astype(BF16)

    fill_own()
    siblings[0].wait_recv()
    fill(BLOCK, BLOCK, 0)
    for side, part in both:
        second[side, part].wait_recv()
        fourth[side, part] = gather(side, part, 1, 3, 2)
    siblings[1] = to_sibling(1)
    for block, arrivals in ((1, None), (2, third), (3, fourth)):
        if arrivals is not None:
            for side, part in both:
                arrivals[side, part].wait_recv()
            siblings[block] = to_sibling(block)
        for start in range(0, block * 512, 1024):
            fill(start, min(1024, block * 512 - start), block)
        siblings[block].wait_recv()
        for column in range(block + 1):
            fill(block * 512, 512, column)

    def grad_p(block, half):
        row = block * 512 + half * BLOCK
        return jnp.dot(coef[row : row + BLOCK, :], rows_q[...], preferred_element_type=F32)

    def grad_q(block):
        return lax.dot_general(
            coef[:, block * BLOCK : (block + 1) * BLOCK], rows_p[...],
            (((0,), (0,)), ((), ())), preferred_element_type=F32,
        )

    sib_sums = {}

    def give_sibling(block):
        rows = pl.ds(block * BLOCK, BLOCK)
        sib_out[rows, :] = grad_p(block, 1)
        sib_sums[block] = send(sib_out.at[rows], sib_in.at[rows], sibling)

    def own_p(block):
        own = grad_p(block, 0)
        sib_sums[block].wait_recv()
        return own + sib_in[pl.ds(block * BLOCK, BLOCK), :]

    def halve(value, out, landing, block, cube):
        start = (block - 2) * BLOCK
        out[pl.ds(start, BLOCK), :] = value.astype(BF16)
        sent = []
        for part, (_, size, offset) in enumerate(PARTS):
            rows = pl.ds(start + offset, 2 * size)
            sent.append(send(out.at[rows], landing.at[rows], cube[(part + 2) % 3]))
        return sent

    sums1 = {}
    for block in (3, 2):
        give_sibling(block)
        sums1[1, block] = halve(grad_q(block), out1_q, in1_q, block, cube_q)
        sums1[0, block] = halve(own_p(block), out1_p, in1_p, block, cube_p)

    def halve_again(side, acc, landed, out, landing, cube):
        for copy in sums1[side, 3]:
            copy.wait_recv()
        out[...] = (acc[pl.ds(BLOCK, BLOCK), :] + landed[pl.ds(BLOCK, BLOCK), :].astype(F32)).astype(BF16)
        sent = []
        for part, (_, size, offset) in enumerate(PARTS):
            rows = pl.ds(offset, 2 * size)
            sent.append(send(out.at[rows], landing.at[rows], cube[(part + 1) % 3]))
        return sent

    give_sibling(1)
    acc_q[pl.ds(BLOCK, BLOCK), :] = grad_q(1)
    acc_p[pl.ds(BLOCK, BLOCK), :] = own_p(1)
    sums2 = {}
    sums2[1] = halve_again(1, acc_q, in1_q, out2_q, in2_q, cube_q)
    sums2[0] = halve_again(0, acc_p, in1_p, out2_p, in2_p, cube_p)
    give_sibling(0)
    acc_q[pl.ds(0, BLOCK), :] = grad_q(0)
    acc_p[pl.ds(0, BLOCK), :] = own_p(0)

    ends = (
        (1, acc_q, in1_q, in2_q, out3_q, in3_q, cube_q, unit_q, norm_q, out_q),
        (0, acc_p, in1_p, in2_p, out3_p, in3_p, cube_p, unit_p, norm_p, out_p),
    )
    sums3 = {}
    for side, acc, in1, in2, out3, in3, cube, _, _, _ in ends:
        for part, (first_row, size, offset) in enumerate(PARTS):
            sums1[side, 2][part].wait_recv()
            sums2[side][part].wait_recv()
            rows = pl.ds(offset, 2 * size)
            total = acc[rows, :] + in1[rows, :].astype(F32) + in2[rows, :].astype(F32)
            acc[rows, :] = total
            mine = pl.ds(first_row, size)
            out3[mine, :] = total[size:].astype(BF16)
            sums3[side, part] = send(out3.at[mine], in3.at[mine], cube[part])
    for side, acc, _, _, _, in3, _, unit, norm, out in ends:
        for part, (first_row, size, offset) in enumerate(PARTS):
            sums3[side, part].wait_recv()
            mine = pl.ds(first_row, size)
            grad = acc[pl.ds(offset, size), :] + in3[mine, :].astype(F32)
            direction = unit[mine, :]
            inner = jnp.sum(direction * grad, axis=1, keepdims=True)
            out[mine, :] = (grad - direction * inner) / norm[mine, :]
    for copy in copies:
        copy.wait_send()


def on_device(protein, text, scale, bias):
    def buffer(rows, kind):
        return pltpu.VMEM((rows, WIDTH), kind)

    result = jax.ShapeDtypeStruct((ROWS, WIDTH), F32)
    return pl.pallas_call(
        kernel,
        out_shape=(result, result),
        in_specs=[pl.BlockSpec(memory_space=pltpu.SMEM)] * 2 + [pl.BlockSpec(memory_space=pl.ANY)] * 2,
        out_specs=[pl.BlockSpec(memory_space=pltpu.VMEM)] * 2,
        scratch_shapes=[
            buffer(ROWS, F32), buffer(ROWS, F32), pltpu.VMEM((ROWS, 1), F32), pltpu.VMEM((ROWS, 1), F32),
            buffer(2048, BF16), buffer(1024, BF16), buffer(2048, BF16),
            buffer(512, F32), buffer(512, F32), buffer(1024, F32), buffer(1024, F32),
            buffer(512, BF16), buffer(512, BF16), buffer(512, BF16), buffer(512, BF16),
            buffer(256, BF16), buffer(256, BF16), buffer(256, BF16), buffer(256, BF16),
            buffer(128, BF16), buffer(128, BF16), buffer(128, BF16), buffer(128, BF16),
            pltpu.SemaphoreType.DMA((2,)),
            pltpu.SemaphoreType.DMA((N_COPIES,)),
            pltpu.SemaphoreType.DMA((N_COPIES,)),
        ],
        compiler_params=pltpu.CompilerParams(
            collective_id=0, has_side_effects=True, vmem_limit_bytes=56 * 1024 * 1024
        ),
    )(scale.reshape(1), bias.reshape(1), protein, text)


def solution(mesh):
    in_specs = (P(("dp", "pair"), None), P(("dp", "pair"), None), P(), P())
    out_specs = (P(("dp", "pair"), None), P(("dp", "pair"), None))
    return jax.shard_map(on_device, mesh=mesh, in_specs=in_specs, out_specs=out_specs, check_vma=False)
```

time: 475 us -> 60.3 us (0.13)
  waiting for transfers between devices: 418 us -> 0 us
  Pallas kernels: 0 us -> 55 us
  matrix products: 26.8 us -> 0 us
  between operations: 15.1 us -> 1.94 us
  other arithmetic: 12.6 us -> 0 us
    reduce_scatter x2 -> x0, waiting for transfers between devices: 230 us -> none  [the longest x1 202 us: on_device(): lax.psum_scatter(partial_q, 'dp', scatter_dimension=0, tiled=True)]
    all_gather x2 -> x0, waiting for transfers between devices: 188 us -> none  [the longest x1 169 us: on_device(): columns = lax.all_gather(unit_qb, 'dp', axis=0, tiled=True)]
    pallas_call x0 -> x1, Pallas kernels: none -> 55 us  [on_device(): pl.pallas_call(kernel, out_shape=(result, result), in_specs=[pl.BlockSpec...]
    dot_general x3 -> x0, matrix products: 26.8 us -> none  [the longest x1 10.7 us: on_device(): lax.dot_general(coef, rows_b, (((0,), (0,)), ((), ())), preferred_element...]
    reduce_sum x4 -> x0, other arithmetic: 4.84 us -> none  [the longest x2 2.52 us: back_norm(): inner = jnp.sum(unit * grad_unit, axis=1, keepdims=True)]
  transfers between devices with their start and end apart: 4 -> 0, of which waited for: 4 -> 0; matrix products, arithmetic and copies ran while one was open for 4% -> 0% of each run, Pallas kernels for 0% -> 0%
where the time goes in v1:
time: 60.3 us; the launch traced here: 59.7 us
  Pallas kernels  55 us (91%)
  local copies, waits for them, and re-layouts  2.74 us (5%)
  between operations  1.94 us (3%)
    pallas_call x1, Pallas kernels, on_device(): pl.pallas_call(kernel, out_shape=(result, result), in_specs=[pl.BlockSpec...  55 us
    unnamed x4, local copies, waits for them, and re-layouts  2.74 us

profile of v1, /device:TPU:0, one launch (start us, length us, event | category | flops | bytes accessed | tf_op | source)
XLA Modules:
  0.0 59.7 jit_solution(4106561152156686145)
XLA Ops:
  1.9 55.0 %shard_map.59 = (f32[128,1024]{1,0:T(8,128)}, f32[128,1024]{1,0:T(8,128)}) custom-call(f32[1]{0:T(128)} %bitcast.2.scale_ref, f32[1]{0:T(128)} %bitcast.3.bias_ref, f32[128,1024]{1,0:T(8,128)} %protein.1, f32[128,1024]{1,0:T(8,128)} %text.1), custom_call_target="tpu_custom_call" | custom-call | tf_op jit(solution)/shard_map/pallas_call | solution.py:241
  57.0 0.0 copy-start
  57.0 1.9 %copy.10 = f32[128,1024]{1,0:T(8,128)} copy(f32[128,1024]{1,0:T(8,128)} %get-tuple-element.4) | data formatting | bytes 1048576
  58.9 0.0 copy-done
  58.9 0.8 %copy.11 = f32[128,1024]{1,0:T(8,128)} copy(f32[128,1024]{1,0:T(8,128)S(1)} %copy-done) | data formatting | bytes 1048576
Async XLA Ops:
  57.0 2.0 %copy-start = (f32[128,1024]{1,0:T(8,128)S(1)}, f32[128,1024]{1,0:T(8,128)}, u32[]{:S(2)}) copy-start(f32[128,1024]{1,0:T(8,128)} %get-tuple-element.5) | copy-start | bytes 1572868

commit v2 on v0

v2 whole, which is shorter than its diff:
```python
import math

import jax
import jax.numpy as jnp
from jax import lax
from jax.experimental import pallas as pl
from jax.experimental.pallas import tpu as pltpu
from jax.sharding import PartitionSpec as P

MESH = pl.DeviceIdType.MESH
F32, BF16 = jnp.float32, jnp.bfloat16
LOG2E = math.log2(math.e)
WIDTH = 1024
ROWS = 128
PARTS = ((0, 48), (48, 48), (96, 32))
PLACE = (0, 1, 2, 4, 3, 5, 6, 7)
N_COPIES = 114


def neighbours():
    dp, pair = lax.axis_index("dp"), lax.axis_index("pair")
    z, x_lo, y = dp // 8, (dp // 4) % 2, dp % 4
    x_hi, core = pair // 2, pair % 2
    x = x_hi * 2 + x_lo

    def device(x, y, z, core):
        return (z * 8 + (x % 2) * 4 + y, (x // 2) * 2 + core)

    def p_flip(i):
        return i + 1 - 2 * (i % 2)

    def q_flip(i):
        return (i + 3 + 2 * (i % 2)) % 4

    def cube(flip):
        dy, dz = flip(y) - y, flip(z) - z
        return (
            device(flip(x), y, z, core),
            device(x, y + (1 - core) * dy, z + core * dz, core),
            device(x, y + core * dy, z + (1 - core) * dz, core),
        )

    return cube(p_flip), cube(q_flip), device(x, y, z, 1 - core)


def kernel(
    scale_ref, bias_ref, protein, text, out_p, out_q,
    unit_p, unit_q, norm_p, norm_q, rows_p, rows_q, coef, early_p, early_q, acc_p, acc_q, own_out, sib_out, sib_in,
    out1_p, out1_q, in1_p, in1_q, out2_p, out2_q, in2_p, in2_q, out3_p, out3_q, in3_p, in3_q,
    load_sem, send_sem, recv_sem,
):
    cube_p, cube_q, sibling = neighbours()
    barrier = pltpu.get_barrier_semaphore()
    for device in (*cube_p, *cube_q, sibling):
        pl.semaphore_signal(barrier, inc=1, device_id=device, device_id_type=MESH)
    load_p = pltpu.make_async_copy(protein, unit_p, load_sem.at[0])
    load_q = pltpu.make_async_copy(text, unit_q, load_sem.at[1])
    load_p.start()
    load_q.start()
    scale, bias = scale_ref[0], bias_ref[0]
    copies = []

    def send(src, dst, device):
        i = len(copies)
        copy = pltpu.make_async_remote_copy(
            src_ref=src, dst_ref=dst, send_sem=send_sem.at[i], recv_sem=recv_sem.at[i],
            device_id=device, device_id_type=MESH,
        )
        copy.start()
        copies.append(copy)
        return copy

    def normalise(load, unit, norm, rows):
        load.wait()
        values = unit[...]
        length = jnp.sqrt(jnp.sum(values * values, axis=1, keepdims=True) + 1e-06)
        values = values / length
        unit[...] = values
        norm[...] = length
        rows[0:ROWS, :] = values.astype(BF16)

    normalise(load_p, unit_p, norm_p, rows_p)
    normalise(load_q, unit_q, norm_q, rows_q)
    pl.semaphore_wait(barrier, 7)

    sides = ((rows_p, 2 * ROWS, cube_p), (rows_q, ROWS, cube_q))
    both = [(side, part) for part in range(3) for side in range(2)]
    arrival, from_sibling = {}, {}

    def pass_on(slot, link):
        for side, part in both:
            pass_part(side, part, slot, link)

    def pass_part(side, part, slot, link):
        rows, stride, cube = sides[side]
        start, size = PARTS[part]
        target = slot + (1 << link)
        arrival[side, part, target] = send(
            rows.at[pl.ds(PLACE[slot] * stride + start, size)],
            rows.at[pl.ds(PLACE[target] * stride + start, size)],
            cube[(part + link) % 3],
        )

    def to_sibling(place, start, size):
        row = place * 2 * ROWS + start
        from_sibling.setdefault(place, []).append(
            send(rows_p.at[pl.ds(row, size)], rows_p.at[pl.ds(row + ROWS, size)], sibling)
        )

    def receive(slot, links=()):
        for side, part in both:
            arrival[side, part, slot].wait_recv()
            if side == 0:
                to_sibling(PLACE[slot], *PARTS[part])
            for link in links[:1]:
                pass_part(side, part, slot, link)
        for link in links[1:]:
            pass_on(slot, link)

    def receive_sibling(*places):
        for place in places:
            for copy in from_sibling[place]:
                copy.wait_recv()

    slope, shift = scale * -LOG2E, bias * -LOG2E

    def dots(row, size, column, width):
        return lax.dot_general(
            rows_p[row : row + size, :], rows_q[column : column + width, :],
            (((1,), (1,)), ((), ())), preferred_element_type=F32,
        )

    def fill(row, end, column, last):
        power = jnp.exp2(dots(row, end - row, column, last - column) * slope + shift)
        coef[row:end, column:last] = (scale / (1.0 + power)).astype(BF16)

    def fill_own():
        values = dots(0, 4 * ROWS, 0, 2 * ROWS) * -slope - shift
        row = lax.broadcasted_iota(jnp.int32, values.shape, 0)
        column = lax.broadcasted_iota(jnp.int32, values.shape, 1)
        sign = jnp.where((row == column) & (row < ROWS), 1.0, -1.0)
        coef[0 : 4 * ROWS, 0 : 2 * ROWS] = (-sign * scale / (1.0 + jnp.exp2(sign * values))).astype(BF16)

    for link in range(3):
        pass_on(0, link)
    to_sibling(0, 0, ROWS)
    receive(1, (1, 2))
    receive(2, (2,))
    receive_sibling(0, 1)
    fill_own()
    receive(4)
    receive(3, (2,))
    receive_sibling(2, 3)
    fill(0, 512, 256, 512)
    fill(512, 1024, 0, 512)
    receive(5)
    fill(0, 1024, 512, 768)
    receive_sibling(4, 5)
    fill(1024, 1536, 0, 768)

    def grad_p(place, start=0, end=8 * ROWS):
        row = place * 2 * ROWS
        return jnp.dot(coef[row : row + 2 * ROWS, start:end], rows_q[start:end, :], preferred_element_type=F32)

    def grad_q(place, start=0, end=16 * ROWS):
        return lax.dot_general(
            coef[start:end, place * ROWS : (place + 1) * ROWS], rows_p[start:end, :],
            (((0,), (0,)), ((), ())), preferred_element_type=F32,
        )

    sib_sums, sums = {}, {}

    def share(place, value):
        rows = pl.ds(place * ROWS, ROWS)
        sib_out[rows, :] = value[ROWS:]
        sib_sums[place] = send(sib_out.at[rows], sib_in.at[rows], sibling)
        own_out[rows, :] = value[:ROWS]

    def own_p(place):
        rows = pl.ds(place * ROWS, ROWS)
        sib_sums[place].wait_recv()
        return own_out[rows, :] + sib_in[rows, :]

    accs = (acc_p, acc_q)
    outs = ((out3_p, out2_p, out1_p), (out3_q, out2_q, out1_q))
    ins = ((in3_p, in2_p, in1_p), (in3_q, in2_q, in1_q))
    cubes = (cube_p, cube_q)

    def give(side, slot, part):
        link = slot.bit_length() - 1
        start, size = PARTS[part]
        rows = pl.ds((slot - (1 << link)) * ROWS + start, size)
        sums[side, slot, part] = send(
            outs[side][link].at[rows], ins[side][link].at[rows], cubes[side][(part + link) % 3]
        )

    def put(side, slot, value):
        link = slot.bit_length() - 1
        outs[side][link][pl.ds((slot - (1 << link)) * ROWS, ROWS), :] = value.astype(BF16)

    def give_all(side, slot):
        for part in range(3):
            give(side, slot, part)

    def total(side, slot, part):
        start, size = PARTS[part]
        rows = pl.ds(slot * ROWS + start, size)
        value = accs[side][rows, :]
        for link in (2, 1, 0):
            if slot < 1 << link:
                sums[side, slot + (1 << link), part].wait_recv()
                value += ins[side][link][rows, :].astype(F32)
        return value

    def add_and_give(side, slot):
        link = slot.bit_length() - 1
        for part, (start, size) in enumerate(PARTS):
            rows = pl.ds((slot - (1 << link)) * ROWS + start, size)
            outs[side][link][rows, :] = total(side, slot, part).astype(BF16)
            give(side, slot, part)

    def keep(side, slot, value):
        accs[side][pl.ds(slot * ROWS, ROWS), :] = value

    def give_p(slot):
        put(0, slot, own_p(PLACE[slot]))
        give_all(0, slot)

    def give_q(slot):
        put(1, slot, grad_q(PLACE[slot]))
        give_all(1, slot)

    early_p[...] = grad_p(5, 0, 768)
    receive(6)
    receive_sibling(6)
    fill(1536, 1792, 0, 768)
    early_q[...] = grad_q(5, 0, 1792)
    receive(7)
    fill(1280, 1536, 768, 1024)
    share(5, early_p[...] + grad_p(5, 768, 1024))
    fill(0, 1024, 768, 1024)
    receive_sibling(7)
    fill(1792, 2048, 0, 1024)
    put(1, 5, early_q[...] + grad_q(5, 1792, 2048))
    give_all(1, 5)
    share(7, grad_p(7))
    give_p(5)
    fill(1024, 1280, 768, 1024)
    fill(1536, 1792, 768, 1024)
    give_q(7)
    share(6, grad_p(6))
    give_p(7)
    give_q(6)
    share(4, grad_p(4))
    give_p(6)
    keep(1, 3, grad_q(4))
    share(3, grad_p(3))
    put(1, 4, grad_q(3))
    keep(0, 3, own_p(4))
    for side in (1, 0):
        add_and_give(side, 3)
    give_all(1, 4)
    give_p(4)
    share(2, grad_p(2))
    keep(1, 2, grad_q(2))
    share(1, grad_p(1))
    keep(0, 2, own_p(2))
    for side in (1, 0):
        add_and_give(side, 2)
    keep(1, 1, grad_q(1))
    share(0, grad_p(0))
    keep(0, 1, own_p(1))
    keep(1, 0, grad_q(0))
    keep(0, 0, own_p(0))
    for side in (1, 0):
        add_and_give(side, 1)
    for side, unit, norm, out in ((1, unit_q, norm_q, out_q), (0, unit_p, norm_p, out_p)):
        for part, (start, size) in enumerate(PARTS):
            rows = pl.ds(start, size)
            grad = total(side, 0, part)
            direction = unit[rows, :]
            inner = jnp.sum(direction * grad, axis=1, keepdims=True)
            out[rows, :] = (grad - direction * inner) / norm[rows, :]
    for copy in copies:
        copy.wait_send()


def on_device(protein, text, scale, bias):
    def buffer(rows, kind):
        return pltpu.VMEM((rows, WIDTH), kind)

    result = pltpu.VMEM((ROWS, WIDTH), F32)
    return pl.pallas_call(
        kernel,
        out_shape=(result, result),
        in_specs=[pl.BlockSpec(memory_space=pltpu.SMEM)] * 2 + [pl.BlockSpec(memory_space=pl.ANY)] * 2,
        out_specs=[pl.BlockSpec(memory_space=pltpu.VMEM)] * 2,
        scratch_shapes=[
            buffer(ROWS, F32), buffer(ROWS, F32), pltpu.VMEM((ROWS, 1), F32), pltpu.VMEM((ROWS, 1), F32),
            buffer(2048, BF16), buffer(1024, BF16), buffer(2048, BF16),
            buffer(2 * ROWS, F32), buffer(ROWS, F32),
            *(buffer(4 * ROWS, F32) for _ in range(2)),
            *(buffer(8 * ROWS, F32) for _ in range(3)),
            *(buffer(4 * ROWS, BF16) for _ in range(4)),
            *(buffer(2 * ROWS, BF16) for _ in range(4)),
            *(buffer(ROWS, BF16) for _ in range(4)),
            pltpu.SemaphoreType.DMA((2,)),
            pltpu.SemaphoreType.DMA((N_COPIES,)),
            pltpu.SemaphoreType.DMA((N_COPIES,)),
        ],
        compiler_params=pltpu.CompilerParams(
            collective_id=0, has_side_effects=True, vmem_limit_bytes=56 * 1024 * 1024
        ),
    )(scale.reshape(1), bias.reshape(1), protein, text)


def solution(mesh):
    in_specs = (P(("dp", "pair"), None), P(("dp", "pair"), None), P(), P())
    out_specs = (P(("dp", "pair"), None), P(("dp", "pair"), None))
    return jax.shard_map(on_device, mesh=mesh, in_specs=in_specs, out_specs=out_specs, check_vma=False)
```

time: 475 us -> 54.2 us (0.11)
  waiting for transfers between devices: 418 us -> 0 us
  Pallas kernels: 0 us -> 49.8 us
  matrix products: 26.8 us -> 0 us
  between operations: 15.1 us -> 1.93 us
  other arithmetic: 12.6 us -> 0 us
    reduce_scatter x2 -> x0, waiting for transfers between devices: 230 us -> none  [the longest x1 202 us: on_device(): lax.psum_scatter(partial_q, 'dp', scatter_dimension=0, tiled=True)]
    all_gather x2 -> x0, waiting for transfers between devices: 188 us -> none  [the longest x1 169 us: on_device(): columns = lax.all_gather(unit_qb, 'dp', axis=0, tiled=True)]
    pallas_call x0 -> x1, Pallas kernels: none -> 49.8 us  [on_device(): pl.pallas_call(kernel, out_shape=(result, result), in_specs=[pl.BlockSpec...]
    dot_general x3 -> x0, matrix products: 26.8 us -> none  [the longest x1 10.7 us: on_device(): lax.dot_general(coef, rows_b, (((0,), (0,)), ((), ())), preferred_element...]
    reduce_sum x4 -> x0, other arithmetic: 4.84 us -> none  [the longest x2 2.52 us: back_norm(): inner = jnp.sum(unit * grad_unit, axis=1, keepdims=True)]
  transfers between devices with their start and end apart: 4 -> 0, of which waited for: 4 -> 0; matrix products, arithmetic and copies ran while one was open for 4% -> 0% of each run, Pallas kernels for 0% -> 0%
where the time goes in v2:
time: 54.2 us; the launch traced here: 53.3 us
  Pallas kernels  49.8 us (92%)
  between operations  1.93 us (4%)
  local copies, waits for them, and re-layouts  1.59 us (3%)
    pallas_call x1, Pallas kernels, on_device(): pl.pallas_call(kernel, out_shape=(result, result), in_specs=[pl.BlockSpec...  49.8 us
    unnamed x2, local copies, waits for them, and re-layouts  1.59 us

profile of v2, /device:TPU:0, one launch (start us, length us, event | category | flops | bytes accessed | tf_op | source)
XLA Modules:
  0.0 53.3 jit_solution(2867335564023324604)
XLA Ops:
  1.9 49.8 %shard_map.59 = (f32[128,1024]{1,0:T(8,128)S(1)}, f32[128,1024]{1,0:T(8,128)S(1)}) custom-call(f32[1]{0:T(128)} %bitcast.2.scale_ref, f32[1]{0:T(128)} %bitcast.3.bias_ref, f32[128,1024]{1,0:T(8,128)} %protein.1, f32[128,1024]{1,0:T(8,128)} %text.1), custom_call_target="tpu_custom_call" | custom-call | tf_op jit(solution)/shard_map/pallas_call | solution.py:293
  51.7 0.8 %copy.8 = f32[128,1024]{1,0:T(8,128)} copy(f32[128,1024]{1,0:T(8,128)S(1)} %get-tuple-element.2) | data formatting | bytes 1048576
  52.5 0.8 %copy.9 = f32[128,1024]{1,0:T(8,128)} copy(f32[128,1024]{1,0:T(8,128)S(1)} %get-tuple-element.3) | data formatting | bytes 1048576

commit v3 on v2

--- a/solution.py
+++ b/solution.py
@@ -15,6 +15,7 @@
 PARTS = ((0, 48), (48, 48), (96, 32))
 PLACE = (0, 1, 2, 4, 3, 5, 6, 7)
 N_COPIES = 114
+TILE = (256, 256)
 
 
 def neighbours():
@@ -131,8 +132,10 @@
         )
 
     def fill(row, end, column, last):
-        power = jnp.exp2(dots(row, end - row, column, last - column) * slope + shift)
-        coef[row:end, column:last] = (scale / (1.0 + power)).astype(BF16)
+        for left in range(column, last, TILE[1]):
+            for top in range(row, end, TILE[0]):
+                power = jnp.exp2(dots(top, TILE[0], left, TILE[1]) * slope + shift)
+                coef[top : top + TILE[0], left : left + TILE[1]] = (scale / (1.0 + power)).astype(BF16)
 
     def fill_own():
         values = dots(0, 4 * ROWS, 0, 2 * ROWS) * -slope - shift
@@ -149,15 +152,11 @@
     receive_sibling(0, 1)
     fill_own()
     receive(4)
+    fill(0, 512, 256, 512)
     receive(3, (2,))
     receive_sibling(2, 3)
-    fill(0, 512, 256, 512)
     fill(512, 1024, 0, 512)
     receive(5)
-    fill(0, 1024, 512, 768)
-    receive_sibling(4, 5)
-    fill(1024, 1536, 0, 768)
-
     def grad_p(place, start=0, end=8 * ROWS):
         row = place * 2 * ROWS
         return jnp.dot(coef[row : row + 2 * ROWS, start:end], rows_q[start:end, :], preferred_element_type=F32)
@@ -230,11 +229,22 @@
         put(1, slot, grad_q(PLACE[slot]))
         give_all(1, slot)
 
+    def both_places(place, store_q):
+        value = grad_p(place)
+        store_q(grad_q(place))
+        share(place, value)
+
+    fill(0, 1024, 512, 768)
+    receive_sibling(4)
+    fill(1024, 1280, 0, 768)
+    receive_sibling(5)
+    fill(1280, 1536, 0, 768)
+    receive(6)
     early_p[...] = grad_p(5, 0, 768)
-    receive(6)
+    early_q[...] = grad_q(5, 0, 1536)
     receive_sibling(6)
     fill(1536, 1792, 0, 768)
-    early_q[...] = grad_q(5, 0, 1792)
+    early_q[...] += grad_q(5, 1536, 1792)
     receive(7)
     fill(1280, 1536, 768, 1024)
     share(5, early_p[...] + grad_p(5, 768, 1024))
@@ -248,32 +258,28 @@
     fill(1024, 1280, 768, 1024)
     fill(1536, 1792, 768, 1024)
     give_q(7)
+    give_p(7)
     share(6, grad_p(6))
-    give_p(7)
     give_q(6)
-    share(4, grad_p(4))
+    both_places(4, lambda value: keep(1, 3, value))
     give_p(6)
-    keep(1, 3, grad_q(4))
-    share(3, grad_p(3))
-    put(1, 4, grad_q(3))
+    both_places(3, lambda value: put(1, 4, value))
+    keep(1, 2, grad_q(2))
+    add_and_give(1, 3)
+    give_all(1, 4)
+    share(2, grad_p(2))
     keep(0, 3, own_p(4))
-    for side in (1, 0):
-        add_and_give(side, 3)
-    give_all(1, 4)
+    add_and_give(0, 3)
     give_p(4)
-    share(2, grad_p(2))
-    keep(1, 2, grad_q(2))
-    share(1, grad_p(1))
+    both_places(1, lambda value: keep(1, 1, value))
+    add_and_give(1, 2)
     keep(0, 2, own_p(2))
-    for side in (1, 0):
-        add_and_give(side, 2)
-    keep(1, 1, grad_q(1))
-    share(0, grad_p(0))
+    add_and_give(0, 2)
+    both_places(0, lambda value: keep(1, 0, value))
+    add_and_give(1, 1)
     keep(0, 1, own_p(1))
-    keep(1, 0, grad_q(0))
     keep(0, 0, own_p(0))
-    for side in (1, 0):
-        add_and_give(side, 1)
+    add_and_give(0, 1)
     for side, unit, norm, out in ((1, unit_q, norm_q, out_q), (0, unit_p, norm_p, out_p)):
         for part, (start, size) in enumerate(PARTS):
             rows = pl.ds(start, size)

time: 54.2 us -> 51.5 us (0.950); the launches traced: 53.3 us -> 51.2 us
  Pallas kernels: 49.8 us -> 47.7 us
    pallas_call x1, Pallas kernels: 49.8 us -> 47.7 us  [on_device(): pl.pallas_call(kernel, out_shape=(result, result), in_specs=[pl.BlockSpec...]
where the time goes in v3:
time: 51.5 us; the launch traced here: 51.2 us
  Pallas kernels  47.7 us (93%)
  between operations  1.93 us (4%)
  local copies, waits for them, and re-layouts  1.59 us (3%)
    pallas_call x1, Pallas kernels, on_device(): pl.pallas_call(kernel, out_shape=(result, result), in_specs=[pl.BlockSpec...  47.7 us
    unnamed x2, local copies, waits for them, and re-layouts  1.59 us

profile of v3, /device:TPU:0, one launch (start us, length us, event | category | flops | bytes accessed | tf_op | source)
XLA Modules:
  0.0 51.2 jit_solution(1608229642725848570)
XLA Ops:
  1.9 47.7 %shard_map.59 = (f32[128,1024]{1,0:T(8,128)S(1)}, f32[128,1024]{1,0:T(8,128)S(1)}) custom-call(f32[1]{0:T(128)} %bitcast.2.scale_ref, f32[1]{0:T(128)} %bitcast.3.bias_ref, f32[128,1024]{1,0:T(8,128)} %protein.1, f32[128,1024]{1,0:T(8,128)} %text.1), custom_call_target="tpu_custom_call" | custom-call | tf_op jit(solution)/shard_map/pallas_call | solution.py:299
  49.6 0.8 %copy.8 = f32[128,1024]{1,0:T(8,128)} copy(f32[128,1024]{1,0:T(8,128)S(1)} %get-tuple-element.2) | data formatting | bytes 1048576
  50.4 0.8 %copy.9 = f32[128,1024]{1,0:T(8,128)} copy(f32[128,1024]{1,0:T(8,128)S(1)} %get-tuple-element.3) | data formatting | bytes 1048576

commit v4 on v3

--- a/solution.py
+++ b/solution.py
@@ -108,15 +108,17 @@
             send(rows_p.at[pl.ds(row, size)], rows_p.at[pl.ds(row + ROWS, size)], sibling)
         )
 
-    def receive(slot, links=()):
-        for side, part in both:
-            arrival[side, part, slot].wait_recv()
-            if side == 0:
-                to_sibling(PLACE[slot], *PARTS[part])
-            for link in links[:1]:
-                pass_part(side, part, slot, link)
-        for link in links[1:]:
-            pass_on(slot, link)
+    def receive(slot, links=(), sides=(0, 1)):
+        for side in sides:
+            for part in range(3):
+                arrival[side, part, slot].wait_recv()
+                for link in links[:1]:
+                    pass_part(side, part, slot, link)
+                if side == 0:
+                    to_sibling(PLACE[slot], *PARTS[part])
+            for link in links[1:]:
+                for part in range(3):
+                    pass_part(side, part, slot, link)
 
     def receive_sibling(*places):
         for place in places:
@@ -244,8 +246,9 @@
     early_q[...] = grad_q(5, 0, 1536)
     receive_sibling(6)
     fill(1536, 1792, 0, 768)
+    receive(7, sides=(0,))
     early_q[...] += grad_q(5, 1536, 1792)
-    receive(7)
+    receive(7, sides=(1,))
     fill(1280, 1536, 768, 1024)
     share(5, early_p[...] + grad_p(5, 768, 1024))
     fill(0, 1024, 768, 1024)
@@ -291,12 +294,23 @@
         copy.wait_send()
 
 
+def store(grad_p, grad_q, out_p, out_q, sem):
+    copies = [
+        pltpu.make_async_copy(grad_p, out_p, sem.at[0]),
+        pltpu.make_async_copy(grad_q, out_q, sem.at[1]),
+    ]
+    for copy in copies:
+        copy.start()
+    for copy in copies:
+        copy.wait()
+
+
 def on_device(protein, text, scale, bias):
     def buffer(rows, kind):
         return pltpu.VMEM((rows, WIDTH), kind)
 
     result = pltpu.VMEM((ROWS, WIDTH), F32)
-    return pl.pallas_call(
+    grads = pl.pallas_call(
         kernel,
         out_shape=(result, result),
         in_specs=[pl.BlockSpec(memory_space=pltpu.SMEM)] * 2 + [pl.BlockSpec(memory_space=pl.ANY)] * 2,
@@ -318,6 +332,14 @@
             collective_id=0, has_side_effects=True, vmem_limit_bytes=56 * 1024 * 1024
         ),
     )(scale.reshape(1), bias.reshape(1), protein, text)
+    return pl.pallas_call(
+        store,
+        out_shape=(jax.ShapeDtypeStruct((ROWS, WIDTH), F32),) * 2,
+        in_specs=[pl.BlockSpec(memory_space=pl.ANY)] * 2,
+        out_specs=[pl.BlockSpec(memory_space=pl.ANY)] * 2,
+        scratch_shapes=[pltpu.SemaphoreType.DMA((2,))],
+        compiler_params=pltpu.CompilerParams(vmem_limit_bytes=4 * 1024 * 1024),
+    )(*grads)
 
 
 def solution(mesh):

time: 51.5 us -> 50.9 us (0.988)
  local copies, waits for them, and re-layouts: 1.59 us -> 0 us
  Pallas kernels: 47.7 us -> 48.6 us
    unnamed x2 -> x0, local copies, waits for them, and re-layouts: 1.59 us -> none
    pallas_call x0 -> x1, Pallas kernels: none -> 0.99 us  [on_device(): pl.pallas_call(store, out_shape=(jax.ShapeDtypeStruct((ROWS, WIDTH), F32)...]
where the time goes in v4:
time: 50.9 us; the launch traced here: 50.7 us
  Pallas kernels  48.6 us (95%)
  between operations  2.09 us (4%)
    pallas_call x1, Pallas kernels, on_device(): pl.pallas_call(kernel, out_shape=(result, result), in_specs=[pl.BlockSpec...  47.6 us

profile of v4, /device:TPU:0, one launch (start us, length us, event | category | flops | bytes accessed | tf_op | source)
XLA Modules:
  0.0 50.7 jit_solution(14573817698561912980)
XLA Ops:
  1.9 47.6 %shard_map.59 = (f32[128,1024]{1,0:T(8,128)S(1)}, f32[128,1024]{1,0:T(8,128)S(1)}) custom-call(f32[1]{0:T(128)} %bitcast.2.scale_ref, f32[1]{0:T(128)} %bitcast.3.bias_ref, f32[128,1024]{1,0:T(8,128)} %protein.1, f32[128,1024]{1,0:T(8,128)} %text.1), custom_call_target="tpu_custom_call" | custom-call | tf_op jit(solution)/shard_map/pallas_call | solution.py:313
  49.5 1.0 %shard_map.60 = (f32[128,1024]{1,0:T(8,128)}, f32[128,1024]{1,0:T(8,128)}) custom-call(f32[128,1024]{1,0:T(8,128)S(1)} %get-tuple-element.4.grad_p, f32[128,1024]{1,0:T(8,128)S(1)} %get-tuple-element.5.grad_q), custom_call_target="tpu_custom_call" | custom-call | tf_op jit(solution)/shard_map/pallas_call | solution.py:335

commit v5 on v4

--- a/solution.py
+++ b/solution.py
@@ -254,9 +254,10 @@
     fill(0, 1024, 768, 1024)
     receive_sibling(7)
     fill(1792, 2048, 0, 1024)
+    value = grad_p(7)
     put(1, 5, early_q[...] + grad_q(5, 1792, 2048))
     give_all(1, 5)
-    share(7, grad_p(7))
+    share(7, value)
     give_p(5)
     fill(1024, 1280, 768, 1024)
     fill(1536, 1792, 768, 1024)
@@ -283,7 +284,7 @@
     keep(0, 1, own_p(1))
     keep(0, 0, own_p(0))
     add_and_give(0, 1)
-    for side, unit, norm, out in ((1, unit_q, norm_q, out_q), (0, unit_p, norm_p, out_p)):
+    for side, unit, norm, out in ((0, unit_p, norm_p, out_p), (1, unit_q, norm_q, out_q)):
         for part, (start, size) in enumerate(PARTS):
             rows = pl.ds(start, size)
             grad = total(side, 0, part)

time: 50.9 us -> 50.5 us (level)
  Pallas kernels: 48.6 us -> 48 us
    pallas_call x1, Pallas kernels: 47.6 us -> 47 us  [on_device(): pl.pallas_call(kernel, out_shape=(result, result), in_specs=[pl.BlockSpec...]
where the time goes in v5:
time: 50.5 us; the launch traced here: 50.1 us
  Pallas kernels  48 us (95%)
  between operations  2.09 us (4%)
    pallas_call x1, Pallas kernels, on_device(): pl.pallas_call(kernel, out_shape=(result, result), in_specs=[pl.BlockSpec...  47 us

profile of v5, /device:TPU:0, one launch (start us, length us, event | category | flops | bytes accessed | tf_op | source)
XLA Modules:
  0.0 50.1 jit_solution(1708231912025991088)
XLA Ops:
  1.9 47.0 %shard_map.59 = (f32[128,1024]{1,0:T(8,128)S(1)}, f32[128,1024]{1,0:T(8,128)S(1)}) custom-call(f32[1]{0:T(128)} %bitcast.2.scale_ref, f32[1]{0:T(128)} %bitcast.3.bias_ref, f32[128,1024]{1,0:T(8,128)} %protein.1, f32[128,1024]{1,0:T(8,128)} %text.1), custom_call_target="tpu_custom_call" | custom-call | tf_op jit(solution)/shard_map/pallas_call | solution.py:314
  48.9 1.0 %shard_map.60 = (f32[128,1024]{1,0:T(8,128)}, f32[128,1024]{1,0:T(8,128)}) custom-call(f32[128,1024]{1,0:T(8,128)S(1)} %get-tuple-element.4.grad_p, f32[128,1024]{1,0:T(8,128)S(1)} %get-tuple-element.5.grad_q), custom_call_target="tpu_custom_call" | custom-call | tf_op jit(solution)/shard_map/pallas_call | solution.py:336

commit v6 on v5

--- a/solution.py
+++ b/solution.py
@@ -282,8 +282,8 @@
     both_places(0, lambda value: keep(1, 0, value))
     add_and_give(1, 1)
     keep(0, 1, own_p(1))
+    add_and_give(0, 1)
     keep(0, 0, own_p(0))
-    add_and_give(0, 1)
     for side, unit, norm, out in ((0, unit_p, norm_p, out_p), (1, unit_q, norm_q, out_q)):
         for part, (start, size) in enumerate(PARTS):
             rows = pl.ds(start, size)

time: 50.5 us -> 50.5 us (level)
  no operation moved by 1% of the time
where the time goes in v6:
time: 50.5 us; the launch traced here: 50.1 us
  Pallas kernels  48 us (95%)
  between operations  2.09 us (4%)
    pallas_call x1, Pallas kernels, on_device(): pl.pallas_call(kernel, out_shape=(result, result), in_specs=[pl.BlockSpec...  47 us

profile of v6, /device:TPU:0, one launch (start us, length us, event | category | flops | bytes accessed | tf_op | source)
XLA Modules:
  0.0 50.1 jit_solution(4899934261173780731)
XLA Ops:
  1.9 47.0 %shard_map.59 = (f32[128,1024]{1,0:T(8,128)S(1)}, f32[128,1024]{1,0:T(8,128)S(1)}) custom-call(f32[1]{0:T(128)} %bitcast.2.scale_ref, f32[1]{0:T(128)} %bitcast.3.bias_ref, f32[128,1024]{1,0:T(8,128)} %protein.1, f32[128,1024]{1,0:T(8,128)} %text.1), custom_call_target="tpu_custom_call" | custom-call | tf_op jit(solution)/shard_map/pallas_call | solution.py:314
  48.9 1.0 %shard_map.60 = (f32[128,1024]{1,0:T(8,128)}, f32[128,1024]{1,0:T(8,128)}) custom-call(f32[128,1024]{1,0:T(8,128)S(1)} %get-tuple-element.4.grad_p, f32[128,1024]{1,0:T(8,128)S(1)} %get-tuple-element.5.grad_q), custom_call_target="tpu_custom_call" | custom-call | tf_op jit(solution)/shard_map/pallas_call | solution.py:336
